TPU v7x, 512 devices: a whole 4x8x8 slice. The times are simulated.
512 devices in a mesh: row: 8 (over z), col: 16 (over y_hi, x, core), kpart: 4 (over y_lo).
Axes of the slice: x: 4, y: 8 (y_hi: 2, y_lo: 4; y = y_hi * 4 + y_lo), z: 8, core: 2. Of those that a mesh axis runs over, the one named last changes fastest.
Arguments:
- left_cyclic: float32 [2048, 8192], P(('kpart', 'col'), 'row'), may hold values from -6 to 6
- right_cyclic: float32 [2048, 16384], P(('kpart', 'row'), 'col'), may hold values from -0.125 to 0.125
Outputs:
- product: float32 [8192, 16384], P(('row', 'kpart'), 'col')
All inputs are finite; a program needn't handle non-finite values.
Results may differ from a plain program's by a relative error of at most 0.00007.
Values sent between devices are 32-bit elements; how exact they have to be, the bound alone decides.
No kernel may reach another device: no remote copies, remote signals or barrier semaphores. Data moves between devices by JAX's collectives and lax.ppermute only.
A program may use at most 64 MiB of HBM per device.

v0:
```python
import jax
import jax.numpy as jnp
from jax import lax
from jax.sharding import PartitionSpec as P

NB = 64


def contract(left_part, right_part):
    return lax.dot_general(
        left_part,
        right_part,
        (((0,), (0,)), ((), ())),
        precision=lax.Precision.HIGHEST,
        preferred_element_type=jnp.float32,
    )


def shards(left_cyclic, right_cyclic):
    row_count = lax.axis_size("row")
    column_count = lax.axis_size("col")
    slab_left, local_rows = left_cyclic.shape
    group_left = local_rows // (NB * row_count)
    shaped_left = left_cyclic.reshape(slab_left, row_count, group_left, 1, NB)
    moved_left = lax.all_to_all(shaped_left, "row", split_axis=1, concat_axis=3, tiled=True)
    band_left = moved_left.reshape(slab_left, local_rows)
    left_band = lax.all_gather(band_left, "col", axis=0, tiled=True)
    slab_right, local_cols = right_cyclic.shape
    group_right = local_cols // (NB * column_count)
    shaped_right = right_cyclic.reshape(slab_right, column_count, group_right, 1, NB)
    moved_right = lax.all_to_all(shaped_right, "col", split_axis=1, concat_axis=3, tiled=True)
    band_right = moved_right.reshape(slab_right, local_cols)
    right_band = lax.all_gather(band_right, "row", axis=0, tiled=True)
    return lax.psum_scatter(
        contract(left_band, right_band), "kpart", scatter_dimension=0, tiled=True
    )


def solution(mesh):
    placed = (P(("kpart", "col"), "row"), P(("kpart", "row"), "col"))
    return jax.shard_map(
        shards, mesh=mesh, in_specs=placed, out_specs=P(("row", "kpart"), "col"), check_vma=False
    )
```

profile of v0, /device:TPU:57, one launch (start us, length us, event | category | flops | bytes accessed | tf_op | source)
XLA Modules:
  0.0 246.7 jit_solution(4141008044242358849)
XLA Ops:
  6.5 1.1 reshape.19
  7.6 0.2 copy.11
  7.8 0.3 reshape.23
  8.2 16.5 %all_to_all.24 = f32[16,1,4096]{2,1,0:T(1,128)S(1)} all-to-all(f32[16,1,4096]{2,1,0:T(1,128)S(1)} %reshape.23), channel_id=1, replica_groups=mesh['row'=8,'col'=16,'kpart'=4] {'col'}, dimensions={0} | all-to-all | bytes 524288 | tf_op jit(solution)/shard_map/all_to_all | solution.py:31
  24.7 0.5 broadcast
  25.2 1.2 reduce.1
  26.5 0.2 reshape.24
  26.7 0.3 copy.8
  27.0 0.9 reshape.20
  27.9 0.0 all-gather.5.cloned.1.call-update
  27.9 0.0 all-gather.3.cloned.1.call-start
  28.0 0.2 reshape.17
  28.2 0.1 copy.12
  28.3 0.3 reshape.21
  28.5 17.6 %all_to_all.25 = f32[8,1,4096]{2,1,0:T(1,128)S(1)} all-to-all(f32[8,1,4096]{2,1,0:T(1,128)S(1)} %reshape.21), channel_id=1, replica_groups=mesh['row'=8,'col'=16,'kpart'=4] {'row'}, dimensions={0} | all-to-all | bytes 262144 | tf_op jit(solution)/shard_map/all_to_all | solution.py:25
  46.1 0.9 reduce
  47.1 0.2 reshape.22
  47.3 0.2 copy.6
  47.5 0.8 reshape.18
  48.3 0.0 reduce-scatter.2.cloned.1.call-start
  48.3 25.2 %all-gather.5.cloned.1.call-done = f32[512,1024]{1,0:T(8,128)} async-done(((f32[64,1024]{1,0:T(8,128)}), f32[512,1024]{1,0:T(8,128)}) %all-gather.5.cloned.1.call-update) | async-done | bytes 2097168 | tf_op jit(solution)/shard_map/all_gather | solution.py:33
  73.5 68.3 %all-gather.3.cloned.1.call-done = f32[512,1024]{1,0:T(8,128)} async-done(((f32[32,1024]{1,0:T(8,128)}), f32[512,1024]{1,0:T(8,128)}) %all-gather.3.cloned.1.call-update) | async-done | bytes 2097168 | tf_op jit(solution)/shard_map/all_gather | solution.py:27
  141.8 10.2 %fusion = f32[1024,1024]{1,0:T(8,128)} fusion(f32[512,1024]{1,0:T(8,128)} %all-gather.3.cloned.1.call-done, f32[512,1024]{1,0:T(8,128)} %all-gather.5.cloned.1.call-done), kind=kOutput, calls=%fused_computation.3 | convolution fusion | flops 6442450944 | bytes 8388608 | tf_op jit(solution)/shard_map/dot_general | solution.py:10
  152.0 88.2 %reduce-scatter.2.cloned.1.call-done = f32[256,1024]{1,0:T(8,128)} async-done(((f32[1024,1024]{1,0:T(8,128)}), f32[256,1024]{1,0:T(8,128)}) %reduce-scatter.2.cloned.1.call-update) | async-done | bytes 1048592 | tf_op jit(solution)/shard_map/reduce_scatter | solution.py:34
  (6 shorter events, 0.1 us)
Async XLA Ops:
  6.5 66.9 %all-gather.5.cloned.1.call-start = ((), (), s32[]{:S(2)}) async-start(), calls=%async_computation.4 | async-start | bytes 2359296 | tf_op jit(solution)/shard_map/all_gather | solution.py:33
  8.1 19.8 %copy-start = (f32[32,1024]{1,0:T(8,128)S(1)}, f32[32,1024]{1,0:T(8,128)}, u32[]{:S(2)}) copy-start(f32[32,1024]{1,0:T(8,128)} %param.2) | copy-start | bytes 393220
  27.9 113.9 %all-gather.3.cloned.1.call-start = ((), (), s32[]{:S(2)}) async-start(), calls=%async_computation.3 | async-start | bytes 2228224 | tf_op jit(solution)/shard_map/all_gather | solution.py:27
  48.3 191.9 %reduce-scatter.2.cloned.1.call-start = ((), (), s32[]{:S(2)}) async-start(), calls=%async_computation.5 | async-start | bytes 5242880 | tf_op jit(solution)/shard_map/reduce_scatter | solution.py:34
Sparse Core Ops, SparseCore 0:
  28.0 45.4 all-gather.4
  76.8 64.9 all-gather.2
  152.1 88.0 reduce-scatter.1
where the time goes:
time: 247 us
  waiting for transfers between devices  182 us (74%)
  blocking collectives  34.1 us (14%)
  between operations  13.2 us (5%)
  matrix products  10.2 us (4%)
  local copies, waits for them, and re-layouts  5.21 us (2%)
    reduce_scatter x1, waiting for transfers between devices, shards(): lax.psum_scatter(contract(left_band, right_band), 'kpart', scatter_dimens...  88.2 us
    all_gather x1, waiting for transfers between devices, shards(): left_band = lax.all_gather(band_left, 'col', axis=0, tiled=True)  68.3 us
    all_gather x1, waiting for transfers between devices, shards(): right_band = lax.all_gather(band_right, 'row', axis=0, tiled=True)  25.2 us
    all_to_all x1, blocking collectives, shards(): lax.all_to_all(shaped_left, 'row', split_axis=1, concat_axis=3, tiled=True)  17.6 us
    all_to_all x1, blocking collectives, shards(): lax.all_to_all(shaped_right, 'col', split_axis=1, concat_axis=3, tiled=True)  16.5 us
    dot_general x1, matrix products, contract(): lax.dot_general(left_part, right_part, (((0,), (0,)), ((), ())), precisio...  10.2 us
  transfers between devices with their start and end apart: 3, of which 3 were waited for; matrix products, arithmetic and copies ran while one was open for 1% of the time, Pallas kernels for 0%

commit v1 on v0

--- a/solution.py
+++ b/solution.py
@@ -4,6 +4,22 @@
 from jax.sharding import PartitionSpec as P
 
 NB = 64
+
+
+def swapped_with_each(array, axis, split, join):
+    ways, here = (lax.axis_size(axis), lax.axis_index(axis))
+    width = array.shape[split] // ways
+    lengths = list(array.shape)
+    lengths[split] = width
+    height = lengths[join]
+    lengths[join] = height * ways
+    full = jnp.zeros(lengths, array.dtype)
+    for mask in range(ways):
+        part = lax.dynamic_slice_in_dim(array, (here ^ mask) * width, width, axis=split)
+        if mask:
+            part = lax.ppermute(part, axis, [(d, d ^ mask) for d in range(ways)])
+        full = lax.dynamic_update_slice_in_dim(full, part, (here ^ mask) * height, axis=join)
+    return full
 
 
 def contract(left_part, right_part):
@@ -22,7 +38,7 @@
     slab_left, local_rows = left_cyclic.shape
     group_left = local_rows // (NB * row_count)
     shaped_left = left_cyclic.reshape(slab_left, row_count, group_left, 1, NB)
-    moved_left = lax.all_to_all(shaped_left, "row", split_axis=1, concat_axis=3, tiled=True)
+    moved_left = swapped_with_each(shaped_left, "row", 1, 3)
     band_left = moved_left.reshape(slab_left, local_rows)
     left_band = lax.all_gather(band_left, "col", axis=0, tiled=True)
     slab_right, local_cols = right_cyclic.shape

time: 247 us -> 257 us (1.040)
  starting transfers between devices: 0.09 us -> 30.2 us
  blocking collectives: 34.1 us -> 19.2 us
  waiting for transfers between devices: 182 us -> 177 us
    ppermute x0 -> x7, starting transfers between devices: none -> 30.2 us  [swapped_with_each(): part = lax.ppermute(part, axis, [(d, d ^ mask) for d in range(ways)])]
    all_gather x1, waiting for transfers between devices: 68.3 us -> 41.2 us  [shards(): left_band = lax.all_gather(band_left, 'col', axis=0, tiled=True)]
    all_gather x1, waiting for transfers between devices: 25.2 us -> 43.8 us  [shards(): right_band = lax.all_gather(band_right, 'row', axis=0, tiled=True)]
    all_to_all x1 -> x0, blocking collectives: 17.6 us -> none  [shards(): lax.all_to_all(shaped_left, 'row', split_axis=1, concat_axis=3, tiled=True)]
    ppermute x0 -> x7, waiting for transfers between devices: none -> 2.77 us  [swapped_with_each(): part = lax.ppermute(part, axis, [(d, d ^ mask) for d in range(ways)])]
    all_to_all x1, blocking collectives: 16.5 us -> 19.2 us  [shards(): lax.all_to_all(shaped_right, 'col', split_axis=1, concat_axis=3, tiled=True)]
  transfers between devices with their start and end apart: 3 -> 10, of which waited for: 3 -> 4; matrix products, arithmetic and copies ran while one was open for 1% -> 2% of each run, Pallas kernels for 0% -> 0%
where the time goes in v1:
time: 257 us
  waiting for transfers between devices  177 us (69%)
  starting transfers between devices  30.2 us (12%)
  blocking collectives  19.2 us (7%)
  between operations  13.4 us (5%)
  matrix products  10.2 us (4%)
  local copies, waits for them, and re-layouts  5.82 us (2%)
    reduce_scatter x1, waiting for transfers between devices, shards(): lax.psum_scatter(contract(left_band, right_band), 'kpart', scatter_dimens...  89.2 us
    all_gather x1, waiting for transfers between devices, shards(): right_band = lax.all_gather(band_right, 'row', axis=0, tiled=True)  43.8 us
    all_gather x1, waiting for transfers between devices, shards(): left_band = lax.all_gather(band_left, 'col', axis=0, tiled=True)  41.2 us
    ppermute x7, starting transfers between devices, swapped_with_each(): part = lax.ppermute(part, axis, [(d, d ^ mask) for d in range(ways)])  30.2 us
    all_to_all x1, blocking collectives, shards(): lax.all_to_all(shaped_right, 'col', split_axis=1, concat_axis=3, tiled=True)  19.2 us
    dot_general x1, matrix products, contract(): lax.dot_general(left_part, right_part, (((0,), (0,)), ((), ())), precisio...  10.2 us
  transfers between devices with their start and end apart: 10, of which 4 were waited for; matrix products, arithmetic and copies ran while one was open for 2% of the time, Pallas kernels for 0%

profile of v1, /device:TPU:57, one launch (start us, length us, event | category | flops | bytes accessed | tf_op | source)
XLA Modules:
  0.0 257.1 jit_solution(710982607109292422)
XLA Ops:
  6.5 1.1 reshape.16
  7.8 5.8 %collective-permute-start.1 = (f32[32,1,2,1,64]{4,3,2,0,1:T(1,128)S(1)}, f32[32,1,2,1,64]{4,3,2,0,1:T(1,128)S(1)}, u32[]{:S(2)}, u32[]{:S(2)}) collective-permute-start(f32[32,1,2,1,64]{4,3,2,0,1:T(1,128)S(1)} %bitcast.31), channel_id=1, source_target_pairs={{0,128},{64,192},{128,0},{192,64},{256,384},{320,448},{384,256},{4... | collective-permute-start | bytes 49160 | tf_op jit(solution)/shard_map/ppermute | solution.py:20
  13.7 4.0 %collective-permute-start = (f32[32,1,2,1,64]{4,3,2,0,1:T(1,128)S(1)}, f32[32,1,2,1,64]{4,3,2,0,1:T(1,128)S(1)}, u32[]{:S(2)}, u32[]{:S(2)}) collective-permute-start(f32[32,1,2,1,64]{4,3,2,0,1:T(1,128)S(1)} %bitcast.30), channel_id=1, source_target_pairs={{0,64},{64,0},{128,192},{192,128},{256,320},{320,256},{384,448},{4... | collective-permute-start | bytes 49160 | tf_op jit(solution)/shard_map/ppermute | solution.py:20
  17.7 6.1 %collective-permute-start.5 = (f32[32,1,2,1,64]{4,3,2,0,1:T(1,128)S(1)}, f32[32,1,2,1,64]{4,3,2,0,1:T(1,128)S(1)}, u32[]{:S(2)}, u32[]{:S(2)}) collective-permute-start(f32[32,1,2,1,64]{4,3,2,0,1:T(1,128)S(1)} %bitcast.26), channel_id=1, source_target_pairs={{0,384},{64,448},{128,256},{192,320},{256,128},{320,192},{384,0},{... | collective-permute-start | bytes 49160 | tf_op jit(solution)/shard_map/ppermute | solution.py:20
  23.8 3.7 %collective-permute-start.3 = (f32[32,1,2,1,64]{4,3,2,0,1:T(1,128)S(1)}, f32[32,1,2,1,64]{4,3,2,0,1:T(1,128)S(1)}, u32[]{:S(2)}, u32[]{:S(2)}) collective-permute-start(f32[32,1,2,1,64]{4,3,2,0,1:T(1,128)S(1)} %bitcast.28), channel_id=1, source_target_pairs={{0,256},{64,320},{128,384},{192,448},{256,0},{320,64},{384,128},{4... | collective-permute-start | bytes 49160 | tf_op jit(solution)/shard_map/ppermute | solution.py:20
  27.5 2.2 collective-permute-start.2
  29.7 6.4 %collective-permute-start.4 = (f32[32,1,2,1,64]{4,3,2,0,1:T(1,128)S(1)}, f32[32,1,2,1,64]{4,3,2,0,1:T(1,128)S(1)}, u32[]{:S(2)}, u32[]{:S(2)}) collective-permute-start(f32[32,1,2,1,64]{4,3,2,0,1:T(1,128)S(1)} %bitcast.27), channel_id=1, source_target_pairs={{0,320},{64,256},{128,448},{192,384},{256,64},{320,0},{384,192},{4... | collective-permute-start | bytes 49160 | tf_op jit(solution)/shard_map/ppermute | solution.py:20
  36.1 1.9 collective-permute-start.6
  38.1 0.2 dynamic_update_slice.24
  38.3 0.2 dynamic_update_slice.25
  39.3 2.8 %collective-permute-done.6 = f32[32,1,2,1,64]{4,3,2,0,1:T(1,128)S(1)} collective-permute-done((f32[32,1,2,1,64]{4,3,2,0,1:T(1,128)S(1)}, f32[32,1,2,1,64]{4,3,2,0,1:T(1,128)S(1)}, u32[]{:S(2)}, u32[]{:S(2)}) %collective-permute-start.6) | collective-permute-done | bytes 16416 | tf_op jit(solution)/shard_map/ppermute | solution.py:20
  42.2 0.8 reshape.17
  43.2 0.2 copy.38
  43.3 0.3 reshape.20
  43.7 19.2 %all_to_all.4 = f32[16,1,4096]{2,1,0:T(1,128)S(1)} all-to-all(f32[16,1,4096]{2,1,0:T(1,128)S(1)} %reshape.20), channel_id=1, replica_groups=mesh['row'=8,'col'=16,'kpart'=4] {'col'}, dimensions={0} | all-to-all | bytes 524288 | tf_op jit(solution)/shard_map/all_to_all | solution.py:47
  62.9 0.5 broadcast
  63.4 1.3 reduce
  64.7 0.2 reshape.21
  64.9 0.3 copy.28
  65.2 0.9 reshape.19
  66.2 41.2 %all-gather.3.cloned.1.call-done = f32[512,1024]{1,0:T(8,128)} async-done(((f32[32,1024]{1,0:T(8,128)}), f32[512,1024]{1,0:T(8,128)}) %all-gather.3.cloned.1.call-update) | async-done | bytes 2097168 | tf_op jit(solution)/shard_map/all_gather | solution.py:43
  107.4 43.8 %all-gather.5.cloned.1.call-done = f32[512,1024]{1,0:T(8,128)} async-done(((f32[64,1024]{1,0:T(8,128)}), f32[512,1024]{1,0:T(8,128)}) %all-gather.5.cloned.1.call-update) | async-done | bytes 2097168 | tf_op jit(solution)/shard_map/all_gather | solution.py:49
  151.2 10.2 %fusion = f32[1024,1024]{1,0:T(8,128)} fusion(f32[512,1024]{1,0:T(8,128)} %all-gather.3.cloned.1.call-done, f32[512,1024]{1,0:T(8,128)} %all-gather.5.cloned.1.call-done), kind=kOutput, calls=%fused_computation.9 | convolution fusion | flops 6442450944 | bytes 8388608 | tf_op jit(solution)/shard_map/dot_general | solution.py:26
  161.5 89.2 %reduce-scatter.2.cloned.1.call-done = f32[256,1024]{1,0:T(8,128)} async-done(((f32[1024,1024]{1,0:T(8,128)}), f32[256,1024]{1,0:T(8,128)}) %reduce-scatter.2.cloned.1.call-update) | async-done | bytes 1048592 | tf_op jit(solution)/shard_map/reduce_scatter | solution.py:50
  (23 shorter events, 1.3 us)
Async XLA Ops:
  6.5 36.5 %copy-start = (f32[64,1024]{1,0:T(8,128)S(1)}, f32[64,1024]{1,0:T(8,128)}, u32[]{:S(2)}) copy-start(f32[64,1024]{1,0:T(8,128)} %param.3) | copy-start | bytes 786436
  6.5 100.9 %all-gather.3.cloned.1.call-start = ((), (), s32[]{:S(2)}) async-start(), calls=%async_computation.2 | async-start | bytes 2228224 | tf_op jit(solution)/shard_map/all_gather | solution.py:43
  7.8 21.9 %collective-permute-start.1 = (f32[32,1,2,1,64]{4,3,2,0,1:T(1,128)S(1)}, f32[32,1,2,1,64]{4,3,2,0,1:T(1,128)S(1)}, u32[]{:S(2)}, u32[]{:S(2)}) collective-permute-start(f32[32,1,2,1,64]{4,3,2,0,1:T(1,128)S(1)} %bitcast.31), channel_id=1, source_target_pairs={{0,128},{64,192},{128,0},{192,64},{256,384},{320,448},{384,256},{4... | collective-permute-start | bytes 49160 | tf_op jit(solution)/shard_map/ppermute | solution.py:20
  13.7 22.5 %collective-permute-start = (f32[32,1,2,1,64]{4,3,2,0,1:T(1,128)S(1)}, f32[32,1,2,1,64]{4,3,2,0,1:T(1,128)S(1)}, u32[]{:S(2)}, u32[]{:S(2)}) collective-permute-start(f32[32,1,2,1,64]{4,3,2,0,1:T(1,128)S(1)} %bitcast.30), channel_id=1, source_target_pairs={{0,64},{64,0},{128,192},{192,128},{256,320},{320,256},{384,448},{4... | collective-permute-start | bytes 49160 | tf_op jit(solution)/shard_map/ppermute | solution.py:20
  17.7 21.4 %collective-permute-start.5 = (f32[32,1,2,1,64]{4,3,2,0,1:T(1,128)S(1)}, f32[32,1,2,1,64]{4,3,2,0,1:T(1,128)S(1)}, u32[]{:S(2)}, u32[]{:S(2)}) collective-permute-start(f32[32,1,2,1,64]{4,3,2,0,1:T(1,128)S(1)} %bitcast.26), channel_id=1, source_target_pairs={{0,384},{64,448},{128,256},{192,320},{256,128},{320,192},{384,0},{... | collective-permute-start | bytes 49160 | tf_op jit(solution)/shard_map/ppermute | solution.py:20
  23.8 15.0 %collective-permute-start.3 = (f32[32,1,2,1,64]{4,3,2,0,1:T(1,128)S(1)}, f32[32,1,2,1,64]{4,3,2,0,1:T(1,128)S(1)}, u32[]{:S(2)}, u32[]{:S(2)}) collective-permute-start(f32[32,1,2,1,64]{4,3,2,0,1:T(1,128)S(1)} %bitcast.28), channel_id=1, source_target_pairs={{0,256},{64,320},{128,384},{192,448},{256,0},{320,64},{384,128},{4... | collective-permute-start | bytes 49160 | tf_op jit(solution)/shard_map/ppermute | solution.py:20
  27.5 11.0 %collective-permute-start.2 = (f32[32,1,2,1,64]{4,3,2,0,1:T(1,128)S(1)}, f32[32,1,2,1,64]{4,3,2,0,1:T(1,128)S(1)}, u32[]{:S(2)}, u32[]{:S(2)}) collective-permute-start(f32[32,1,2,1,64]{4,3,2,0,1:T(1,128)S(1)} %bitcast.29), channel_id=1, source_target_pairs={{0,192},{64,128},{128,64},{192,0},{256,448},{320,384},{384,320},{4... | collective-permute-start | bytes 49160 | tf_op jit(solution)/shard_map/ppermute | solution.py:20
  29.7 9.2 %collective-permute-start.4 = (f32[32,1,2,1,64]{4,3,2,0,1:T(1,128)S(1)}, f32[32,1,2,1,64]{4,3,2,0,1:T(1,128)S(1)}, u32[]{:S(2)}, u32[]{:S(2)}) collective-permute-start(f32[32,1,2,1,64]{4,3,2,0,1:T(1,128)S(1)} %bitcast.27), channel_id=1, source_target_pairs={{0,320},{64,256},{128,448},{192,384},{256,64},{320,0},{384,192},{4... | collective-permute-start | bytes 49160 | tf_op jit(solution)/shard_map/ppermute | solution.py:20
  36.1 5.9 %collective-permute-start.6 = (f32[32,1,2,1,64]{4,3,2,0,1:T(1,128)S(1)}, f32[32,1,2,1,64]{4,3,2,0,1:T(1,128)S(1)}, u32[]{:S(2)}, u32[]{:S(2)}) collective-permute-start(f32[32,1,2,1,64]{4,3,2,0,1:T(1,128)S(1)} %bitcast.25), channel_id=1, source_target_pairs={{0,448},{64,384},{128,320},{192,256},{256,192},{320,128},{384,64},... | collective-permute-start | bytes 49160 | tf_op jit(solution)/shard_map/ppermute | solution.py:20
  43.0 108.3 %all-gather.5.cloned.1.call-start = ((), (), s32[]{:S(2)}) async-start(), calls=%async_computation.3 | async-start | bytes 2359296 | tf_op jit(solution)/shard_map/all_gather | solution.py:49
  66.1 184.5 %reduce-scatter.2.cloned.1.call-start = ((), (), s32[]{:S(2)}) async-start(), calls=%async_computation.4 | async-start | bytes 5242880 | tf_op jit(solution)/shard_map/reduce_scatter | solution.py:50
Sparse Core Ops, SparseCore 0:
  43.1 64.2 all-gather.2
  109.5 41.7 all-gather.4
  161.6 88.9 reduce-scatter.1
